TPU v7x, 256 devices: a whole 4x4x8 slice. The times are simulated.
256 devices in a mesh: layer: 64 (over z, x_lo, y), shot: 4 (over x_hi, core).
Axes of the slice: x: 4 (x_hi: 2, x_lo: 2; x = x_hi * 2 + x_lo), y: 4, z: 8, core: 2. Of those that a mesh axis runs over, the one named last changes fastest.
Arguments:
- residual_src: bfloat16 [8, 192, 48, 1536], P('shot', 'layer'), may hold values from -6 to 6
- src_plane: int32 [8], P('shot'), may hold values from 0 to 191
- src_shift: int32 [8], P('shot'), may hold values from 0 to 767
- profile: bfloat16 [8, 48, 1536], P('shot'), may hold values from -6 to 6
- mass: bfloat16 [192, 48, 768], P('layer'), may hold values from 0.049804688 to 1
- damping: bfloat16 [192, 48, 768], P('layer'), may hold values from 0.049804688 to 0.5
- panel: bfloat16 [64, 1536, 1536], P('layer', None, 'shot'), may hold values from -0.15625 to 0.15625
- transmission: float32 [64, 48, 1536], P('layer'), may hold values from -1 to 1, as said below
Outputs:
- solution: bfloat16 [8, 192, 48, 1536], P('shot', 'layer')
Inputs may be any that keep to these rules, and one draw needn't show every extreme that they name: `transmission`: each cell's complex factor, real part in the first 768 columns and imaginary part in the last 768, has magnitude below one.
All inputs are finite; a program needn't handle non-finite values.
Results may differ from a plain program's by a relative error of at most 0.0045.
Values may be sent and summed in bfloat16 or wider, within the bound.
A program may use at most 192 MiB of HBM per device.

v0:
```python
import jax
import jax.numpy as jnp
from jax import lax
from jax.sharding import PartitionSpec as P

relaxation = 0.8


def prefix(value, axis, join, neutral):
    count, mine = (lax.axis_size(axis), lax.axis_index(axis))
    pieces = jax.tree.map(lambda part: lax.all_gather(part, axis), value)
    subtotal = jax.tree.map(
        lambda part, zero: jnp.full_like(part, 0) + jnp.asarray(zero, part.dtype), value, neutral
    )

    def hop(position, subtotal):
        longer = join(subtotal, jax.tree.map(lambda part: part[position], pieces))
        return jax.tree.map(lambda new, old: jnp.where(position < mine, new, old), longer, subtotal)

    return lax.fori_loop(0, count - 1, hop, subtotal)


def as_sent(array):
    return jax.tree.map(lambda a: a.astype(jnp.bfloat16) if a.dtype == jnp.float32 else a, array)


def padded_2(block, sides, width):
    for axis, dim in sides:
        count = lax.axis_size(axis)
        forward = [(i, i + 1) for i in range(count - 1)]
        backward = [(target, source) for source, target in forward]
        low = lax.ppermute(
            lax.slice_in_dim(block, block.shape[dim] - width, None, axis=dim), axis, forward
        )
        high = lax.ppermute(lax.slice_in_dim(block, 0, width, axis=dim), axis, backward)
        block = jnp.concatenate([low, block, high], axis=dim)
    return block


def complex_mul(first_op, second_op):
    half_width = first_op.shape[-1] // 2
    real_one = first_op[..., :half_width]
    imag_one = first_op[..., half_width:]
    real_two = second_op[..., :half_width]
    imag_two = second_op[..., half_width:]
    return jnp.concatenate(
        [real_one * real_two - imag_one * imag_two, real_one * imag_two + imag_one * real_two],
        axis=-1,
    )


def lateral_smooth(values):
    half_width = values.shape[-1] // 2
    split_view = values.reshape(values.shape[:-1] + (2, half_width))
    padded = jnp.pad(split_view, [(0, 0)] * (split_view.ndim - 1) + [(1, 1)])
    along_x = 0.5 * padded[..., :-2] + padded[..., 1:-1] + 0.5 * padded[..., 2:]
    along_x = along_x.reshape(values.shape)
    padded_y = jnp.pad(along_x, [(0, 0)] * (values.ndim - 2) + [(1, 1), (0, 0)])
    return 0.5 * padded_y[..., :-2, :] + padded_y[..., 1:-1, :] + 0.5 * padded_y[..., 2:, :]


def depth_smooth(padded, axis_pos):
    inner_count = padded.shape[axis_pos] - 2
    above_part = lax.slice_in_dim(padded, 0, inner_count, axis=axis_pos)
    middle = lax.slice_in_dim(padded, 1, inner_count + 1, axis=axis_pos)
    below_part = lax.slice_in_dim(padded, 2, inner_count + 2, axis=axis_pos)
    return 0.5 * above_part + middle + 0.5 * below_part


def coefficients(mass_val, damp_val):
    shifted = 1.0 + mass_val
    modulus = shifted * shifted + damp_val * damp_val
    diag_coef = jnp.concatenate([shifted, damp_val], axis=-1)
    inverse = jnp.concatenate([shifted / modulus, -damp_val / modulus], axis=-1)
    return (diag_coef, inverse)


def jacobi_update(iterate, smoothed, source_field, diag_coef, inverse):
    residual_now = source_field - complex_mul(diag_coef, iterate) + (smoothed - iterate) / 7.0
    return iterate + relaxation * complex_mul(inverse, residual_now)


def carry_trace(bottom_field, transmission):
    factor = transmission[0]
    half_width = factor.shape[-1] // 2
    unit_factor = jnp.concatenate(
        [jnp.ones_like(factor[:, :half_width]), jnp.zeros_like(factor[:, half_width:])], axis=-1
    )

    def compose(earlier_pair, later_pair):
        return (
            complex_mul(later_pair[0], earlier_pair[0]),
            complex_mul(later_pair[0][None], earlier_pair[1]) + later_pair[1],
        )

    composed = prefix(
        (factor, bottom_field), "layer", compose, (unit_factor, jnp.zeros_like(bottom_field))
    )
    return composed[1]


def on_device(residual_src, src_plane, src_shift, profile, mass, damping, panel, transmission):
    shot_count, planes_dev, lat_rows, full_width = residual_src.shape
    half_width = full_width // 2
    group_idx = lax.axis_index("layer")
    plane_ids = group_idx * planes_dev + jnp.arange(planes_dev, dtype=jnp.int32)

    def roll_one(shot_profile, shift_id):
        return jnp.roll(
            shot_profile.astype(jnp.float32).reshape(lat_rows, 2, half_width), shift_id, axis=2
        ).reshape(lat_rows, full_width)

    shifted_profile = jax.vmap(roll_one)(profile, src_shift)
    on_plane = (plane_ids[None, :] == src_plane[:, None]).astype(jnp.float32)
    forcing = (
        residual_src.astype(jnp.float32) + on_plane[:, :, None, None] * shifted_profile[:, None]
    ).astype(jnp.bfloat16)
    flat_src = forcing.reshape(-1, full_width)
    product = jnp.dot(
        flat_src,
        lax.all_gather(panel, "shot", axis=2, tiled=True)[0],
        preferred_element_type=jnp.float32,
    )
    panel_field = forcing.astype(jnp.float32) + product.reshape(forcing.shape)
    incoming = carry_trace(panel_field[:, planes_dev - 1], transmission)
    source_field = jnp.concatenate(
        [panel_field[:, :1] + incoming[:, None], panel_field[:, 1:]], axis=1
    )
    diag_coef, inverse = coefficients(mass.astype(jnp.float32), damping.astype(jnp.float32))
    iterate = relaxation * complex_mul(inverse, source_field)
    padded = padded_2(as_sent(iterate), (("layer", 1),), 1).astype(iterate.dtype)
    smoothed = depth_smooth(lateral_smooth(padded), 1)
    iterate = jacobi_update(iterate, smoothed, source_field, diag_coef, inverse)
    return iterate.astype(jnp.bfloat16)


def solution(mesh):
    placed = (
        P("shot", "layer", None, None),
        P("shot"),
        P("shot"),
        P("shot", None, None),
        P("layer", None, None),
        P("layer", None, None),
        P("layer", None, "shot"),
        P("layer", None, None),
    )
    return jax.shard_map(
        on_device,
        mesh=mesh,
        in_specs=placed,
        out_specs=P("shot", "layer", None, None),
        check_vma=False,
    )
```

profile of v0, /device:TPU:1, one launch (start us, length us, event | category | flops | bytes accessed | tf_op | source)
XLA Modules:
  0.0 1000.7 jit_solution(10149514813066162594)
XLA Ops:
  9.1 1.8 copy.25
  11.0 6.2 maximum_convert_fusion
  17.1 3.8 gather_fusion
  20.9 2.5 copy.27
  24.0 33.4 %all-gather.5.cloned.1.call-done = bf16[1,1536,1536]{2,1,0:T(8,128)(2,1)} async-done(((bf16[1,1536,384]{2,1,0:T(8,128)(2,1)}), bf16[1,1536,1536]{2,1,0:T(8,128)(2,1)}) %all-gather.5.cloned.1.call-update) | async-done | bytes 4718608 | tf_op jit(solution)/shard_map/all_gather | solution.py:121
  57.4 4.4 fusion.12
  65.1 289.7 %all-gather.7.cloned.1.call-done = f32[64,48,1536]{2,1,0:T(8,128)} async-done(((f32[1,48,1536]{2,1,0:T(8,128)}), f32[64,48,1536]{2,1,0:T(8,128)}) %all-gather.7.cloned.1.call-update) | async-done | bytes 18874384 | tf_op jit(solution)/shard_map/all_gather | solution.py:11
  354.9 456.8 %all-gather.9.cloned.1.call-done = f32[128,1,48,1536]{3,2,1,0:T(8,128)} async-done(((f32[2,1,48,1536]{3,2,1,0:T(8,128)}), f32[128,1,48,1536]{3,2,1,0:T(8,128)}) %all-gather.9.cloned.1.call-update) | async-done | bytes 37748752 | tf_op jit(solution)/shard_map/all_gather | solution.py:11
  811.6 157.6 %while.14 = (s32[]{:T(128)}, f32[2,48,1536]{2,1,0:T(8,128)S(1)}, s32[]{:T(128)}, f32[64,48,1536]{2,1,0:T(8,128)}, f32[64,2,48,1536]{3,2,1,0:T(8,128)}, /*index=5*/s32[]{:T(128)}, s32[]{:T(128)}, s32[]{}) while((s32[]{:T(128)}, f32[2,48,1536]{2,1,0:T(8,128)S(1)}, s32[]{:T(128)}, f32[64,48,1536]{2,1,0:T(8,128)}, ...), condition=%wide.region_1.2_spmd.clone, body=%wide.region_0.1_spmd.clone.sunk | while | flops 1179653 | bytes 5603458 | solution.py:20
  812.8 1.3 fusion.33
  815.3 1.3 fusion.33
  817.8 1.3 fusion.33
  820.3 1.3 fusion.33
  822.8 1.3 fusion.33
  825.3 1.3 fusion.33
  827.8 1.3 fusion.33
  852.8 1.3 fusion.33
  855.3 1.3 fusion.33
  857.8 1.3 fusion.33
  860.3 1.3 fusion.33
  862.8 1.3 fusion.33
  865.3 1.3 fusion.33
  867.8 1.3 fusion.33
  971.8 2.0 collective-permute-start
  973.8 1.5 collective-permute-start.1
  976.4 1.5 multiply_subtract_fusion.2
  979.1 1.7 concatenate.51
  980.8 1.7 copy.28
  982.6 1.4 collective-permute-done.1
  983.9 1.7 concatenate.55
  986.7 1.5 maximum_convert_fusion.1
  988.1 1.6 fusion.6
  (292 shorter events, 152.7 us)
Async XLA Ops:
  6.5 4.4 copy-start.12
  6.5 50.9 %all-gather.5.cloned.1.call-start = ((), (), s32[]{:S(2)}) async-start(), calls=%async_computation | async-start | bytes 5898240 | tf_op jit(solution)/shard_map/all_gather | solution.py:121
  7.3 347.6 %all-gather.7.cloned.1.call-start = ((), (), s32[]{:S(2)}) async-start(), calls=%async_computation.1 | async-start | bytes 19169280 | tf_op jit(solution)/shard_map/all_gather | solution.py:11
  8.0 803.6 %all-gather.9.cloned.1.call-start = ((), (), s32[]{:S(2)}) async-start(), calls=%async_computation.2 | async-start | bytes 38338560 | tf_op jit(solution)/shard_map/all_gather | solution.py:11
  20.9 3.0 copy-start.11
  61.8 3.2 copy-start.6
  61.9 1.2 copy-start.9
  61.9 2.0 copy-start.10
  969.2 1.2 copy-start
  969.2 1.3 copy-start.2
  971.0 5.3 copy-start.7
  971.1 5.3 copy-start.8
  971.8 7.3 collective-permute-start
  973.8 10.1 %collective-permute-start.1 = (bf16[2,1,48,1536]{3,2,1,0:T(8,128)(2,1)}, bf16[2,1,48,1536]{3,2,1,0:T(8,128)(2,1)}, u32[]{:S(2)}, u32[]{:S(2)}) collective-permute-start(bf16[2,1,48,1536]{3,2,1,0:T(8,128)(2,1)} %get-tuple-element.141), channel_id=1, source_target_pairs={{4,0},{8,4},{12,8},{16,12},{20,16},{24,20},{28,24},{32,28},{36,32}... | collective-permute-start | bytes 884744 | tf_op jit(solution)/shard_map/ppermute | solution.py:35
  990.1 1.2 copy-start.4
  990.1 1.4 copy-start.5
  991.6 1.0 copy-start.1
  991.6 1.1 copy-start.3
Sparse Core Ops, SparseCore 0:
  9.2 48.1 all-gather.4
  59.2 295.6 all-gather.6
  356.6 454.9 all-gather.8
where the time goes:
time: 1010 us; the launch traced here: 1000 us
  waiting for transfers between devices  784 us (78%)
  other arithmetic  110 us (11%)
  local copies, waits for them, and re-layouts  83 us (8%)
  between operations  13.3 us (1%)
    all_gather x2, waiting for transfers between devices, prefix(): pieces = jax.tree.map(lambda part: lax.all_gather(part, axis), value)  746 us
    select_n x63, other arithmetic, hop(): jnp.where(position < mine, new, old)  84.1 us
    mul x63, local copies, waits for them, and re-layouts, complex_mul(): real_one * real_two - imag_one * imag_two  63.6 us
    all_gather x1, waiting for transfers between devices, on_device(): lax.all_gather(panel, 'shot', axis=2, tiled=True)[0]  33.4 us
  transfers between devices with their start and end apart: 5, of which 5 were waited for; matrix products, arithmetic and copies ran while one was open for 3% of the time, Pallas kernels for 0%

commit v1 on v0

v1 whole, which is shorter than its diff:
```python
import jax
import jax.numpy as jnp
from jax import lax
from jax.experimental import pallas as pl
from jax.experimental.pallas import tpu as pltpu
from jax.sharding import PartitionSpec as P

MESH = pl.DeviceIdType.MESH
F32, BF16 = jnp.float32, jnp.bfloat16
RELAX = 0.8
NY, NX, W, LZ = 48, 768, 1536, 3
ROWS = 2 * NY
COLS = 384
HALF = 384
NT = 9
NPOS = 16


def forcing_kernel(plane_ref, shift_ref, res_ref, prof_ref, out_ref):
    first = lax.axis_index("layer") * LZ
    for shot in range(2):
        rows = pl.ds(shot * NY, NY)
        for p in range(LZ):
            out_ref[p, rows] = res_ref[shot, p]
        at = plane_ref[shot] - first

        @pl.when((at >= 0) & (at < LZ))
        def _():
            for half in range(2):
                cols = pl.ds(half * NX, NX)
                rolled = pltpu.roll(prof_ref[shot, :, cols].astype(F32), shift_ref[shot], axis=1)
                out_ref[at, rows, cols] = (res_ref[shot, at, :, cols].astype(F32) + rolled).astype(BF16)


def cmul(ar, ai, br, bi):
    return ar * br - ai * bi, ar * bi + ai * br


def lateral(w):
    col = lax.broadcasted_iota(jnp.int32, w.shape, 1)
    row = lax.broadcasted_iota(jnp.int32, w.shape, 0)
    left = jnp.where(col == 0, 0.0, pltpu.roll(w, 1, axis=1))
    right = jnp.where(col == w.shape[1] - 1, 0.0, pltpu.roll(w, w.shape[1] - 1, axis=1))
    w = w + 0.5 * (left + right)
    up = jnp.where(row == 0, 0.0, pltpu.roll(w, 1, axis=0))
    down = jnp.where(row == w.shape[0] - 1, 0.0, pltpu.roll(w, w.shape[0] - 1, axis=0))
    return w + 0.5 * (up + down)


def sweep_kernel(
    f_hbm, mass_hbm, damp_hbm, panel_hbm, trans_hbm, out_hbm,
    pan, fa, rs, rr, md, coef, tv, ty, tblk, ttile, ot,
    pf2, bq, by, tot, ob, ibs, inb, ins, inc, va, hs, hr, outv,
    loc, f_s, f_r, r_s, r_r, md_s, md_r, ty_s, ty_r, tt_s, tt_r,
    by_s, by_r, tot_s, tot_r, ib_s, ib_r, in_s, in_r, h_s, h_r, out_s,
):
    layer, s = lax.axis_index("layer"), lax.axis_index("shot")
    nl = 64
    z, xl, y = layer // 8, (layer // 4) % 2, layer % 4
    xh, core = s // 2, s % 2
    pos = layer // 4

    def rel(k):
        c = (core + k % 2) % 2
        x = (xh + k // 2) % 2
        return x * 2 + c

    def shot_dev(k):
        return (layer, rel(k))

    def y_at(d):
        return (y + d) % 4

    def y_dev(d):
        return ((layer // 4) * 4 + y_at(d), s)

    def pos_dev(p):
        return (p * 4 + y, s)

    def owner(t):
        zt = t % 8
        return zt * 2 + (t + t // 8 + core) % 2

    has_low = (z + core) % 2 == xl
    own_tile = jnp.where(has_low, z, 8)
    owns = has_low | (z == 0)

    up_dev = ((layer + 1) % nl, s)
    dn_dev = ((layer + nl - 1) % nl, s)

    def remote(src, dst, ss, rsem, dev):
        return pltpu.make_async_remote_copy(
            src_ref=src, dst_ref=dst, send_sem=ss, recv_sem=rsem, device_id=dev, device_id_type=MESH
        )

    my_half = pl.multiple_of((y % 2) * HALF, 128)
    loads = [
        pltpu.make_async_copy(panel_hbm.at[0], pan, loc.at[0]),
        pltpu.make_async_copy(f_hbm, fa.at[0], loc.at[1]),
        pltpu.make_async_copy(trans_hbm.at[0], tv, loc.at[2]),
        pltpu.make_async_copy(mass_hbm, md.at[0, pl.ds(0, LZ)], loc.at[3]),
        pltpu.make_async_copy(damp_hbm, md.at[1, pl.ds(0, LZ)], loc.at[4]),
        pltpu.make_async_copy(trans_hbm.at[0, :, pl.ds(my_half, HALF)], ty.at[y, 0], loc.at[5]),
        pltpu.make_async_copy(trans_hbm.at[0, :, pl.ds(NX + my_half, HALF)], ty.at[y, 1], loc.at[6]),
    ]
    for c in loads:
        c.start()

    barrier = pltpu.get_barrier_semaphore()
    greet = [shot_dev(k) for k in (1, 2, 3)] + [y_dev(d) for d in (1, 2, 3)]
    greet += [up_dev, dn_dev]
    greet += [pos_dev((pos + d) % NPOS) for d in range(1, NPOS)]
    for dev in greet:
        pl.semaphore_signal(barrier, inc=1, device_id=dev, device_id_type=MESH)
    pl.semaphore_wait(barrier, len(greet))

    def f_partner(p):
        return remote(f_hbm.at[p], fa.at[2, p], f_s.at[p, 1], f_r.at[p, 1], shot_dev(2))

    def f_sibling(p):
        return remote(f_hbm.at[p], fa.at[1, p], f_s.at[p, 0], f_r.at[p, 0], shot_dev(1))

    def f_forward(p):
        return remote(fa.at[2, p], fa.at[3, p], f_s.at[p, 2], f_r.at[p, 2], shot_dev(1))

    def r_back(p, k):
        return remote(rs.at[k, p], rr.at[p, s], r_s.at[p, k - 1], r_r.at[p, k - 1], shot_dev(k))

    order = (2, 0, 1)
    f_partner(2).start()
    for p in order:
        f_sibling(p).start()

    def t_send(d):
        off = pl.multiple_of((y_at(d) % 2) * HALF, 128)
        return [
            remote(trans_hbm.at[0, :, pl.ds(off + part * NX, HALF)], ty.at[y, part],
                   ty_s.at[d - 1, part], ty_r.at[d - 1, part], y_dev(d))
            for part in range(2)
        ]

    t_sends = [c for d in (1, 2, 3) for c in t_send(d)]
    for c in t_sends:
        c.start()
    md_sends = [
        remote(mass_hbm.at[0], md.at[0, LZ], md_s.at[0], md_r.at[0], dn_dev),
        remote(damp_hbm.at[0], md.at[1, LZ], md_s.at[1], md_r.at[1], dn_dev),
    ]
    for c in md_sends:
        c.start()

    loads[0].wait()
    loads[1].wait()

    def product(slot, planes):
        lhs = fa[slot, planes]
        m = lhs.shape[0] * ROWS if lhs.ndim == 3 else ROWS
        return jnp.dot(lhs.reshape(m, W), pan[...], preferred_element_type=F32).astype(BF16)

    own = product(0, slice(0, LZ))
    for p in range(LZ):
        rr[p, s] = own[p * ROWS:(p + 1) * ROWS]
    for p in order:
        f_sibling(p).wait_recv()
    sib = product(1, slice(0, LZ))
    for p in order:
        rs[1, p] = sib[p * ROWS:(p + 1) * ROWS]
        r_back(p, 1).start()

    loads[3].wait()
    loads[4].wait()

    def coefficients(p):
        sh = 1.0 + md[0, p].astype(F32)
        dm = md[1, p].astype(F32)
        w = RELAX / (sh * sh + dm * dm)
        coef[p, 0] = w * sh
        coef[p, 1] = -(w * dm)

    for p in range(LZ):
        coefficients(p)

    def exchange(p, following):
        f_partner(p).wait_recv()
        if following is not None:
            f_partner(p).wait_send()
            f_partner(following).start()
        f_forward(p).start()
        rs[2, p] = product(2, p)
        r_back(p, 2).start()
        f_forward(p).wait_recv()
        rs[3, p] = product(3, p)
        r_back(p, 3).start()

    exchange(2, 0)

    loads[2].wait()
    loads[5].wait()
    loads[6].wait()
    for c in t_sends:
        c.wait_recv()
    tr, ti = ty[0, 0], ty[0, 1]
    for j in range(1, 4):
        tr, ti = cmul(ty[j, 0], ty[j, 1], tr, ti)
    tblk[0] = tr
    tblk[1] = ti
    for t in range(NT):
        rt, ct = pl.ds((t // 3) * 16, 16), pl.ds((t % 3) * 128, 128)
        for part in range(2):
            ttile[t, part] = tblk[part, rt, ct]

    def tile_send(t, src, dst, ss, rsem):
        @pl.when(owner(t) != pos)
        def _():
            remote(src.at[t], dst.at[pos], ss.at[t], rsem.at[pos], pos_dev(owner(t))).start()

        @pl.when(owner(t) == pos)
        def _():
            dst[pos] = src[t]

    def tile_sent(t, src, dst, ss, rsem):
        @pl.when(owner(t) != pos)
        def _():
            remote(src.at[t], dst.at[pos], ss.at[t], rsem.at[pos], pos_dev(owner(t))).wait_send()

    def tile_recv(src, dst, ss, rsem):
        for q in range(NPOS):
            @pl.when(pos != q)
            def _():
                remote(src.at[0], dst.at[q], ss.at[0], rsem.at[q], pos_dev(q)).wait_recv()

    for t in range(NT):
        tile_send(t, ttile, ot, tt_s, tt_r)

    def field(p, shot, part):
        rows = pl.ds(shot * NY, NY)
        f = fa[0, p, rows, pl.ds(part * NX, NX)].astype(F32)
        prod = jnp.concatenate([rr[p, part * 2, rows], rr[p, part * 2 + 1, rows]], axis=-1)
        return f + prod.astype(F32)

    for k in (1, 2, 3):
        r_back(2, k).wait_recv()
    for shot in range(2):
        rows = pl.ds(shot * NY, NY)
        re, im = field(2, shot, 0), field(2, shot, 1)
        pf2[rows, pl.ds(0, NX)] = re
        pf2[rows, pl.ds(NX, NX)] = im
        for c in range(2):
            cut = slice(c * HALF, (c + 1) * HALF)
            bq[shot * 2 + c, :, pl.ds(0, HALF)] = re[:, cut].astype(BF16)
            bq[shot * 2 + c, :, pl.ds(HALF, HALF)] = im[:, cut].astype(BF16)

    def b_send(d):
        return remote(bq.at[y_at(d)], by.at[y], by_s.at[d - 1], by_r.at[d - 1], y_dev(d))

    for d in (1, 2, 3):
        b_send(d).start()
    by[y] = bq[y]

    def local_iterate(p, slot):
        for shot in range(2):
            rows = pl.ds(shot * NY, NY)
            if p == 2:
                re, im = pf2[rows, pl.ds(0, NX)], pf2[rows, pl.ds(NX, NX)]
            else:
                re, im = field(p, shot, 0), field(p, shot, 1)
            vr, vi = cmul(coef[p, 0], coef[p, 1], re, im)
            va[p + 1, rows, pl.ds(0, NX)] = vr
            va[p + 1, rows, pl.ds(NX, NX)] = vi
            if slot is not None:
                hs[slot, rows, pl.ds(0, NX)] = vr.astype(BF16)
                hs[slot, rows, pl.ds(NX, NX)] = vi.astype(BF16)

    local_iterate(2, 0)
    halo_down = remote(hs.at[0], hr.at[0], h_s.at[0], h_r.at[0], up_dev)
    halo_up = remote(hs.at[1], hr.at[1], h_s.at[1], h_r.at[1], dn_dev)
    halo_down.start()

    exchange(0, 1)

    for d in (1, 2, 3):
        b_send(d).wait_recv()
    re, im = by[0, :, pl.ds(0, HALF)].astype(F32), by[0, :, pl.ds(HALF, HALF)].astype(F32)
    for j in range(1, 4):
        re, im = cmul(ty[j, 0], ty[j, 1], re, im)
        re = re + by[j, :, pl.ds(0, HALF)].astype(F32)
        im = im + by[j, :, pl.ds(HALF, HALF)].astype(F32)
    for t in range(NT):
        rt, ct = slice((t // 3) * 16, (t // 3) * 16 + 16), slice((t % 3) * 128, (t % 3) * 128 + 128)
        tot[t, 0] = re[rt, ct].astype(BF16)
        tot[t, 1] = im[rt, ct].astype(BF16)
    for t in range(NT):
        tile_send(t, tot, ob, tot_s, tot_r)

    for k in (1, 2, 3):
        r_back(0, k).wait_recv()
    local_iterate(0, 1)
    halo_up.start()

    exchange(1, None)

    def back(q):
        return remote(ibs.at[q], inb.at[own_tile], ib_s.at[q], ib_r.at[own_tile], pos_dev(q))

    @pl.when(owns)
    def _():
        tile_recv(ttile, ot, tt_s, tt_r)
        tile_recv(tot, ob, tot_s, tot_r)
        cr = jnp.zeros((16, 128), F32)
        ci = jnp.zeros((16, 128), F32)
        for q in range(NPOS):
            ibs[q, 0] = cr.astype(BF16)
            ibs[q, 1] = ci.astype(BF16)

            @pl.when(pos != q)
            def _():
                back(q).start()

            if q < NPOS - 1:
                cr, ci = cmul(ot[q, 0], ot[q, 1], cr, ci)
                cr = cr + ob[q, 0].astype(F32)
                ci = ci + ob[q, 1].astype(F32)
        inb[own_tile] = ibs[pos]

    for k in (1, 2, 3):
        r_back(1, k).wait_recv()
    local_iterate(1, None)

    for c in md_sends:
        c.wait_recv()
    coefficients(LZ)

    for t in range(NT):
        @pl.when(owner(t) != pos)
        def _():
            remote(ibs.at[0], inb.at[t], ib_s.at[0], ib_r.at[t], pos_dev(owner(t))).wait_recv()
    parts = [
        jnp.concatenate(
            [jnp.concatenate([inb[rt * 3 + ct, part] for ct in range(3)], axis=-1) for rt in range(3)], axis=0
        ).astype(F32)
        for part in range(2)
    ]
    re, im = parts
    for j in range(4):
        ins[j, :, pl.ds(0, HALF)] = re.astype(BF16)
        ins[j, :, pl.ds(HALF, HALF)] = im.astype(BF16)
        if j < 3:
            re, im = cmul(ty[j, 0], ty[j, 1], re, im)
            re = re + by[j, :, pl.ds(0, HALF)].astype(F32)
            im = im + by[j, :, pl.ds(HALF, HALF)].astype(F32)

    def in_send(d):
        return remote(ins.at[y_at(d)], inc.at[y], in_s.at[d - 1], in_r.at[d - 1], y_dev(d))

    for d in (1, 2, 3):
        in_send(d).start()
    inc[y] = ins[y]

    halo_down.wait_recv()
    halo_up.wait_recv()
    not_first = jnp.where(layer == 0, 0.0, 1.0).astype(F32)
    not_last = jnp.where(layer == nl - 1, 0.0, 1.0).astype(F32)
    va[0] = hr[0].astype(F32) * not_first

    for d in (1, 2, 3):
        in_send(d).wait_recv()
    for shot in range(2):
        rows = pl.ds(shot * NY, NY)
        re = jnp.concatenate([inc[shot * 2 + c, :, pl.ds(0, HALF)] for c in range(2)], axis=-1).astype(F32)
        im = jnp.concatenate([inc[shot * 2 + c, :, pl.ds(HALF, HALF)] for c in range(2)], axis=-1).astype(F32)
        vr, vi = cmul(coef[0, 0], coef[0, 1], re, im)
        rcols, icols = pl.ds(0, NX), pl.ds(NX, NX)
        va[1, rows, rcols] += vr
        va[1, rows, icols] += vi
        nr, ni = cmul(tv[:, rcols], tv[:, icols], re, im)
        nr = nr + pf2[rows, rcols]
        ni = ni + pf2[rows, icols]
        vr, vi = cmul(coef[LZ, 0], coef[LZ, 1], nr, ni)
        va[4, rows, rcols] = (vr + hr[1, rows, rcols].astype(F32)) * not_last
        va[4, rows, icols] = (vi + hr[1, rows, icols].astype(F32)) * not_last

    outs = []
    for p in range(LZ):
        for shot in range(2):
            rows = pl.ds(shot * NY, NY)
            diff = []
            for part in range(2):
                cols = pl.ds(part * NX, NX)
                mid = va[p + 1, rows, cols]
                w = mid + 0.5 * (va[p, rows, cols] + va[p + 2, rows, cols])
                diff.append(lateral(w) - mid)
            dr, di = cmul(coef[p, 0], coef[p, 1], diff[0], diff[1])
            outv[shot, p, :, pl.ds(0, NX)] = (1.2 * va[p + 1, rows, pl.ds(0, NX)] + dr * (1.0 / 7.0)).astype(BF16)
            outv[shot, p, :, pl.ds(NX, NX)] = (1.2 * va[p + 1, rows, pl.ds(NX, NX)] + di * (1.0 / 7.0)).astype(BF16)
            c = pltpu.make_async_copy(outv.at[shot, p], out_hbm.at[shot, p], out_s.at[shot, p])
            c.start()
            outs.append(c)

    for p in order:
        if p == 1:
            f_partner(p).wait_send()
        f_sibling(p).wait_send()
        f_forward(p).wait_send()
        for k in (1, 2, 3):
            r_back(p, k).wait_send()
    for c in t_sends + md_sends + [halo_down, halo_up]:
        c.wait_send()
    for d in (1, 2, 3):
        b_send(d).wait_send()
        in_send(d).wait_send()
    for t in range(NT):
        tile_sent(t, ttile, ot, tt_s, tt_r)
        tile_sent(t, tot, ob, tot_s, tot_r)

    @pl.when(owns)
    def _():
        for q in range(NPOS):
            @pl.when(pos != q)
            def _():
                back(q).wait_send()

    for c in outs:
        c.wait()


def on_device(residual_src, src_plane, src_shift, profile, mass, damping, panel, transmission):
    vmem = pl.BlockSpec(memory_space=pltpu.VMEM)
    smem = pl.BlockSpec(memory_space=pltpu.SMEM)
    hbm = pl.BlockSpec(memory_space=pl.ANY)
    forcing = pl.pallas_call(
        forcing_kernel,
        out_shape=jax.ShapeDtypeStruct((LZ, ROWS, W), BF16),
        in_specs=[smem, smem, vmem, vmem],
        out_specs=vmem,
        name="forcing",
        compiler_params=pltpu.CompilerParams(vmem_limit_bytes=16 * 2**20),
    )(src_plane, src_shift, residual_src, profile)
    dma = pltpu.SemaphoreType.DMA
    scratch = [
        pltpu.VMEM((W, COLS), BF16),
        pltpu.VMEM((4, LZ, ROWS, W), BF16),
        pltpu.VMEM((4, LZ, ROWS, COLS), BF16),
        pltpu.VMEM((LZ, 4, ROWS, COLS), BF16),
        pltpu.VMEM((2, LZ + 1, NY, NX), BF16),
        pltpu.VMEM((LZ + 1, 2, NY, NX), F32),
        pltpu.VMEM((NY, W), F32),
        pltpu.VMEM((4, 2, NY, HALF), F32),
        pltpu.VMEM((2, NY, HALF), F32),
        pltpu.VMEM((NT, 2, 16, 128), F32),
        pltpu.VMEM((NPOS, 2, 16, 128), F32),
        pltpu.VMEM((ROWS, W), F32),
        pltpu.VMEM((4, NY, NX), BF16),
        pltpu.VMEM((4, NY, NX), BF16),
        pltpu.VMEM((NT, 2, 16, 128), BF16),
        pltpu.VMEM((NPOS, 2, 16, 128), BF16),
        pltpu.VMEM((NPOS, 2, 16, 128), BF16),
        pltpu.VMEM((NT, 2, 16, 128), BF16),
        pltpu.VMEM((4, NY, NX), BF16),
        pltpu.VMEM((4, NY, NX), BF16),
        pltpu.VMEM((5, ROWS, W), F32),
        pltpu.VMEM((2, ROWS, W), BF16),
        pltpu.VMEM((2, ROWS, W), BF16),
        pltpu.VMEM((2, LZ, NY, W), BF16),
        dma((7,)), dma((LZ, 3)), dma((LZ, 3)), dma((LZ, 3)), dma((LZ, 3)), dma((2,)), dma((2,)),
        dma((3, 2)), dma((3, 2)), dma((NT,)), dma((NPOS,)),
        dma((3,)), dma((3,)), dma((NT,)), dma((NPOS,)), dma((NPOS,)), dma((NT,)),
        dma((3,)), dma((3,)), dma((2,)), dma((2,)), dma((2, LZ)),
    ]
    return pl.pallas_call(
        sweep_kernel,
        out_shape=jax.ShapeDtypeStruct((2, LZ, NY, W), BF16),
        in_specs=[hbm] * 5,
        out_specs=hbm,
        scratch_shapes=scratch,
        name="sweep",
        compiler_params=pltpu.CompilerParams(
            collective_id=0, has_side_effects=True, vmem_limit_bytes=40 * 2**20
        ),
    )(forcing, mass, damping, panel, transmission)


def solution(mesh):
    placed = (
        P("shot", "layer", None, None),
        P("shot"),
        P("shot"),
        P("shot", None, None),
        P("layer", None, None),
        P("layer", None, None),
        P("layer", None, "shot"),
        P("layer", None, None),
    )
    return jax.shard_map(
        on_device,
        mesh=mesh,
        in_specs=placed,
        out_specs=P("shot", "layer", None, None),
        check_vma=False,
    )
```

time: 1010 us -> 78 us (0.08)
  waiting for transfers between devices: 784 us -> 0 us
  other arithmetic: 110 us -> 0 us
  local copies, waits for them, and re-layouts: 83 us -> 4.81 us
  Pallas kernels: 0 us -> 72.2 us
  between operations: 13.3 us -> 0.03 us
    all_gather x3 -> x0, waiting for transfers between devices: 780 us -> none  [the longest x2 746 us: prefix(): pieces = jax.tree.map(lambda part: lax.all_gather(part, axis), value)]
    select_n x63 -> x0, other arithmetic: 84.1 us -> none  [hop(): jnp.where(position < mine, new, old)]
    pallas_call x0 -> x2, Pallas kernels: none -> 72.2 us  [the longest x1 71.4 us: on_device(): pl.pallas_call(sweep_kernel, out_shape=jax.ShapeDtypeStruct((2, LZ, NY, W...]
    mul x64 -> x0, local copies, waits for them, and re-layouts: 64.1 us -> none  [the longest x63 63.6 us: complex_mul(): real_one * real_two - imag_one * imag_two]
  transfers between devices with their start and end apart: 5 -> 0, of which waited for: 5 -> 0; matrix products, arithmetic and copies ran while one was open for 3% -> 0% of each run, Pallas kernels for 0% -> 0%
where the time goes in v1:
time: 78 us; the launch traced here: 77 us
  Pallas kernels  72.2 us (93%)
  local copies, waits for them, and re-layouts  4.81 us (6%)
    pallas_call x1, Pallas kernels, on_device(): pl.pallas_call(sweep_kernel, out_shape=jax.ShapeDtypeStruct((2, LZ, NY, W...  71.4 us
    unnamed x17, local copies, waits for them, and re-layouts  4.81 us

profile of v1, /device:TPU:1, one launch (start us, length us, event | category | flops | bytes accessed | tf_op | source)
XLA Modules:
  0.0 77.0 jit_solution(17213785890402296773)
XLA Ops:
  0.0 0.0 copy-start
  0.0 0.0 copy-start.1
  0.0 1.3 %copy-done.1 = bf16[2,3,48,1536]{3,2,1,0:T(8,128)(2,1)S(1)} copy-done((bf16[2,3,48,1536]{3,2,1,0:T(8,128)(2,1)S(1)}, bf16[2,3,48,1536]{3,2,1,0:T(8,128)(2,1)}, u32[]{:S(2)}) %copy-start.1) | copy-done | bytes 884760
  1.3 0.0 copy-start.2
  1.3 1.0 %copy-done.2 = bf16[2,48,1536]{2,1,0:T(8,128)(2,1)S(1)} copy-done((bf16[2,48,1536]{2,1,0:T(8,128)(2,1)S(1)}, bf16[2,48,1536]{2,1,0:T(8,128)(2,1)}, u32[]{:S(2)}) %copy-start.2) | copy-done | bytes 294936
  2.2 0.0 copy-start.6
  2.2 0.7 copy-done.6
  2.9 0.0 copy-start.7
  2.9 0.7 copy-done.7
  3.5 0.0 copy-start.3
  3.5 0.0 copy-start.4
  3.5 0.0 copy-start.5
  3.5 0.8 forcing.1.f_hbm
  4.3 0.0 copy-done
  4.3 0.2 copy-done.3
  4.5 0.1 copy-done.4
  4.6 0.1 copy-done.5
  4.7 71.4 %sweep.1 = bf16[2,3,48,1536]{3,2,1,0:T(8,128)(2,1)S(1)} custom-call(bf16[3,96,1536]{2,1,0:T(8,128)(2,1)S(1)} %forcing.1.f_hbm, bf16[3,48,768]{2,1,0:T(8,128)(2,1)S(1)} %copy-done.4, bf16[3,48,768]{2,1,0:T(8,128)(2,1)S(1)} %copy-done.5, bf16[1,1536,384]{2,1,0:T(8,128)(2,1)S(1)} %copy-done, f32[1,48,1536]{2,1,0:T(8,128)S(1)} %copy-done.3), custom_call_target="tpu_custom_call" | custom-call | tf_op jit(solution)/shard_map/sweep/pallas_call | solution.py:469
  76.1 0.9 %copy.10 = bf16[2,3,48,1536]{3,2,1,0:T(8,128)(2,1)} copy(bf16[2,3,48,1536]{3,2,1,0:T(8,128)(2,1)S(1)} %sweep.1) | data formatting | bytes 1769472
Async XLA Ops:
  0.0 4.3 %copy-start = (bf16[1,1536,384]{2,1,0:T(8,128)(2,1)S(1)}, bf16[1,1536,384]{2,1,0:T(8,128)(2,1)}, u32[]{:S(2)}) copy-start(bf16[1,1536,384]{2,1,0:T(8,128)(2,1)} %panel_hbm.1) | copy-start | bytes 3538948
  0.0 1.3 %copy-start.1 = (bf16[2,3,48,1536]{3,2,1,0:T(8,128)(2,1)S(1)}, bf16[2,3,48,1536]{3,2,1,0:T(8,128)(2,1)}, u32[]{:S(2)}) copy-start(bf16[2,3,48,1536]{3,2,1,0:T(8,128)(2,1)} %res_ref.1) | copy-start | bytes 2654212
  1.3 1.0 %copy-start.2 = (bf16[2,48,1536]{2,1,0:T(8,128)(2,1)S(1)}, bf16[2,48,1536]{2,1,0:T(8,128)(2,1)}, u32[]{:S(2)}) copy-start(bf16[2,48,1536]{2,1,0:T(8,128)(2,1)} %prof_ref.1) | copy-start | bytes 884740
  2.2 0.7 copy-start.6
  2.9 0.7 copy-start.7
  3.5 1.0 %copy-start.3 = (f32[1,48,1536]{2,1,0:T(8,128)S(1)}, f32[1,48,1536]{2,1,0:T(8,128)}, u32[]{:S(2)}) copy-start(f32[1,48,1536]{2,1,0:T(8,128)} %trans_hbm.1) | copy-start | bytes 884740
  3.5 1.0 %copy-start.4 = (bf16[3,48,768]{2,1,0:T(8,128)(2,1)S(1)}, bf16[3,48,768]{2,1,0:T(8,128)(2,1)}, u32[]{:S(2)}) copy-start(bf16[3,48,768]{2,1,0:T(8,128)(2,1)} %mass_hbm.1) | copy-start | bytes 663556
  3.5 1.1 %copy-start.5 = (bf16[3,48,768]{2,1,0:T(8,128)(2,1)S(1)}, bf16[3,48,768]{2,1,0:T(8,128)(2,1)}, u32[]{:S(2)}) copy-start(bf16[3,48,768]{2,1,0:T(8,128)(2,1)} %damp_hbm.1) | copy-start | bytes 663556

commit v2 on v1

--- a/solution.py
+++ b/solution.py
@@ -8,6 +8,7 @@
 MESH = pl.DeviceIdType.MESH
 F32, BF16 = jnp.float32, jnp.bfloat16
 RELAX = 0.8
+TT = BF16
 NY, NX, W, LZ = 48, 768, 1536, 3
 ROWS = 2 * NY
 COLS = 384
@@ -16,20 +17,10 @@
 NPOS = 16
 
 
-def forcing_kernel(plane_ref, shift_ref, res_ref, prof_ref, out_ref):
-    first = lax.axis_index("layer") * LZ
-    for shot in range(2):
-        rows = pl.ds(shot * NY, NY)
-        for p in range(LZ):
-            out_ref[p, rows] = res_ref[shot, p]
-        at = plane_ref[shot] - first
-
-        @pl.when((at >= 0) & (at < LZ))
-        def _():
-            for half in range(2):
-                cols = pl.ds(half * NX, NX)
-                rolled = pltpu.roll(prof_ref[shot, :, cols].astype(F32), shift_ref[shot], axis=1)
-                out_ref[at, rows, cols] = (res_ref[shot, at, :, cols].astype(F32) + rolled).astype(BF16)
+def rolled(x, shift):
+    for k in range(10):
+        x = jnp.where((shift >> k) & 1 == 1, pltpu.roll(x, 1 << k, axis=1), x)
+    return x
 
 
 def cmul(ar, ai, br, bi):
@@ -48,8 +39,8 @@
 
 
 def sweep_kernel(
-    f_hbm, mass_hbm, damp_hbm, panel_hbm, trans_hbm, out_hbm,
-    pan, fa, rs, rr, md, coef, tv, ty, tblk, ttile, ot,
+    plane_ref, shift_ref, res_hbm, prof_hbm, mass_hbm, damp_hbm, panel_hbm, trans_hbm, out_hbm,
+    resv, profv, pan, fa, rs, rr, md, coef, tv, ty, tblk, ttile, ot,
     pf2, bq, by, tot, ob, ibs, inb, ins, inc, va, hs, hr, outv,
     loc, f_s, f_r, r_s, r_r, md_s, md_r, ty_s, ty_r, tt_s, tt_r,
     by_s, by_r, tot_s, tot_r, ib_s, ib_r, in_s, in_r, h_s, h_r, out_s,
@@ -95,13 +86,14 @@
 
     my_half = pl.multiple_of((y % 2) * HALF, 128)
     loads = [
-        pltpu.make_async_copy(panel_hbm.at[0], pan, loc.at[0]),
-        pltpu.make_async_copy(f_hbm, fa.at[0], loc.at[1]),
-        pltpu.make_async_copy(trans_hbm.at[0], tv, loc.at[2]),
-        pltpu.make_async_copy(mass_hbm, md.at[0, pl.ds(0, LZ)], loc.at[3]),
-        pltpu.make_async_copy(damp_hbm, md.at[1, pl.ds(0, LZ)], loc.at[4]),
-        pltpu.make_async_copy(trans_hbm.at[0, :, pl.ds(my_half, HALF)], ty.at[y, 0], loc.at[5]),
-        pltpu.make_async_copy(trans_hbm.at[0, :, pl.ds(NX + my_half, HALF)], ty.at[y, 1], loc.at[6]),
+        pltpu.make_async_copy(prof_hbm, profv, loc.at[0]),
+        pltpu.make_async_copy(res_hbm, resv, loc.at[1]),
+        pltpu.make_async_copy(panel_hbm.at[0], pan, loc.at[2]),
+        pltpu.make_async_copy(trans_hbm.at[0], tv, loc.at[3]),
+        pltpu.make_async_copy(mass_hbm, md.at[0, pl.ds(0, LZ)], loc.at[4]),
+        pltpu.make_async_copy(damp_hbm, md.at[1, pl.ds(0, LZ)], loc.at[5]),
+        pltpu.make_async_copy(trans_hbm.at[0, :, pl.ds(my_half, HALF)], ty.at[y, 0], loc.at[6]),
+        pltpu.make_async_copy(trans_hbm.at[0, :, pl.ds(NX + my_half, HALF)], ty.at[y, 1], loc.at[7]),
     ]
     for c in loads:
         c.start()
@@ -112,24 +104,50 @@
     greet += [pos_dev((pos + d) % NPOS) for d in range(1, NPOS)]
     for dev in greet:
         pl.semaphore_signal(barrier, inc=1, device_id=dev, device_id_type=MESH)
+
+    first = layer * LZ
+
+    def forcing(p):
+        for shot in range(2):
+            here = plane_ref[shot] == first + p
+            for half in range(2):
+                cols = pl.ds(half * NX, NX)
+                f = resv[shot, p, :, cols].astype(F32)
+                fa[0, p, shot, :, cols] = jnp.where(here, f + va[0, pl.ds(shot * NY, NY), cols], f).astype(BF16)
+
+    loads[0].wait()
+    for shot in range(2):
+        for half in range(2):
+            cols = pl.ds(half * NX, NX)
+            va[0, pl.ds(shot * NY, NY), cols] = rolled(profv[shot, :, cols].astype(F32), shift_ref[shot])
+    loads[1].wait()
+    forcing(2)
     pl.semaphore_wait(barrier, len(greet))
 
-    def f_partner(p):
-        return remote(f_hbm.at[p], fa.at[2, p], f_s.at[p, 1], f_r.at[p, 1], shot_dev(2))
+    def f_partner(p, shot=None):
+        if shot is None:
+            return remote(fa.at[0, p], fa.at[2, p], f_s.at[p, 1, 0], f_r.at[p, 1, 0], shot_dev(2))
+        return remote(fa.at[0, p, shot], fa.at[2, p, shot], f_s.at[p, 1, shot], f_r.at[p, 1, shot], shot_dev(2))
 
     def f_sibling(p):
-        return remote(f_hbm.at[p], fa.at[1, p], f_s.at[p, 0], f_r.at[p, 0], shot_dev(1))
-
-    def f_forward(p):
-        return remote(fa.at[2, p], fa.at[3, p], f_s.at[p, 2], f_r.at[p, 2], shot_dev(1))
-
-    def r_back(p, k):
-        return remote(rs.at[k, p], rr.at[p, s], r_s.at[p, k - 1], r_r.at[p, k - 1], shot_dev(k))
+        return remote(fa.at[0, p], fa.at[1, p], f_s.at[p, 0, 0], f_r.at[p, 0, 0], shot_dev(1))
+
+    def f_forward(p, shot=None):
+        if shot is None:
+            return remote(fa.at[2, p], fa.at[3, p], f_s.at[p, 2, 0], f_r.at[p, 2, 0], shot_dev(1))
+        return remote(fa.at[2, p, shot], fa.at[3, p, shot], f_s.at[p, 2, shot], f_r.at[p, 2, shot], shot_dev(1))
+
+    def r_back(p, k, shot=None):
+        if shot is None:
+            return remote(rs.at[k, p], rr.at[p, s], r_s.at[p, k - 1, 0], r_r.at[p, k - 1, 0], shot_dev(k))
+        return remote(
+            rs.at[k, p, shot], rr.at[p, s, shot], r_s.at[p, k - 1, shot], r_r.at[p, k - 1, shot], shot_dev(k)
+        )
 
     order = (2, 0, 1)
-    f_partner(2).start()
-    for p in order:
-        f_sibling(p).start()
+    for shot in range(2):
+        f_partner(2, shot).start()
+    f_sibling(2).start()
 
     def t_send(d):
         off = pl.multiple_of((y_at(d) % 2) * HALF, 128)
@@ -142,33 +160,48 @@
     t_sends = [c for d in (1, 2, 3) for c in t_send(d)]
     for c in t_sends:
         c.start()
-    md_sends = [
-        remote(mass_hbm.at[0], md.at[0, LZ], md_s.at[0], md_r.at[0], dn_dev),
-        remote(damp_hbm.at[0], md.at[1, LZ], md_s.at[1], md_r.at[1], dn_dev),
-    ]
-    for c in md_sends:
-        c.start()
-
-    loads[0].wait()
-    loads[1].wait()
-
-    def product(slot, planes):
-        lhs = fa[slot, planes]
-        m = lhs.shape[0] * ROWS if lhs.ndim == 3 else ROWS
-        return jnp.dot(lhs.reshape(m, W), pan[...], preferred_element_type=F32).astype(BF16)
-
+    for p in (0, 1):
+        forcing(p)
+        f_sibling(p).start()
+
+    def product(slot, planes, shot=None):
+        lhs = fa[slot, planes] if shot is None else fa[slot, planes, shot]
+        shape = lhs.shape[:-1] + (COLS,)
+        out = jnp.dot(lhs.reshape(-1, W), pan[...], preferred_element_type=F32).astype(BF16)
+        return out.reshape(shape)
+
+    loads[2].wait()
     own = product(0, slice(0, LZ))
     for p in range(LZ):
-        rr[p, s] = own[p * ROWS:(p + 1) * ROWS]
+        rr[p, s] = own[p]
     for p in order:
         f_sibling(p).wait_recv()
     sib = product(1, slice(0, LZ))
     for p in order:
-        rs[1, p] = sib[p * ROWS:(p + 1) * ROWS]
+        rs[1, p] = sib[p]
         r_back(p, 1).start()
 
-    loads[3].wait()
+    def exchange(p, shot=None):
+        f_partner(p, shot).wait_recv()
+        f_forward(p, shot).start()
+        where = (p,) if shot is None else (p, shot)
+        rs[(2,) + where] = product(2, p, shot)
+        r_back(p, 2, shot).start()
+
+    def exchange_far(p, shot=None):
+        f_forward(p, shot).wait_recv()
+        where = (p,) if shot is None else (p, shot)
+        rs[(3,) + where] = product(3, p, shot)
+        r_back(p, 3, shot).start()
+
+    exchange(2, 0)
+    exchange_far(2, 0)
+    exchange(2, 1)
+    f_partner(0).start()
+    exchange_far(2, 1)
+
     loads[4].wait()
+    loads[5].wait()
 
     def coefficients(p):
         sh = 1.0 + md[0, p].astype(F32)
@@ -177,26 +210,9 @@
         coef[p, 0] = w * sh
         coef[p, 1] = -(w * dm)
 
-    for p in range(LZ):
-        coefficients(p)
-
-    def exchange(p, following):
-        f_partner(p).wait_recv()
-        if following is not None:
-            f_partner(p).wait_send()
-            f_partner(following).start()
-        f_forward(p).start()
-        rs[2, p] = product(2, p)
-        r_back(p, 2).start()
-        f_forward(p).wait_recv()
-        rs[3, p] = product(3, p)
-        r_back(p, 3).start()
-
-    exchange(2, 0)
-
-    loads[2].wait()
-    loads[5].wait()
+    loads[3].wait()
     loads[6].wait()
+    loads[7].wait()
     for c in t_sends:
         c.wait_recv()
     tr, ti = ty[0, 0], ty[0, 1]
@@ -233,28 +249,38 @@
         tile_send(t, ttile, ot, tt_s, tt_r)
 
     def field(p, shot, part):
-        rows = pl.ds(shot * NY, NY)
-        f = fa[0, p, rows, pl.ds(part * NX, NX)].astype(F32)
-        prod = jnp.concatenate([rr[p, part * 2, rows], rr[p, part * 2 + 1, rows]], axis=-1)
+        f = fa[0, p, shot, :, pl.ds(part * NX, NX)].astype(F32)
+        prod = jnp.concatenate([rr[p, part * 2, shot], rr[p, part * 2 + 1, shot]], axis=-1)
         return f + prod.astype(F32)
 
-    for k in (1, 2, 3):
-        r_back(2, k).wait_recv()
+    def b_send(i):
+        return remote(bq.at[i], by.at[y], by_s.at[i], by_r.at[y], ((layer // 4) * 4 + i, s))
+
+    def on_others(n, mine, action):
+        for i in range(n):
+            @pl.when(mine != i)
+            def _(i=i):
+                action(i)
+
     for shot in range(2):
         rows = pl.ds(shot * NY, NY)
+        if shot == 0:
+            r_back(2, 1).wait_recv()
+        for k in (2, 3):
+            r_back(2, k, shot).wait_recv()
         re, im = field(2, shot, 0), field(2, shot, 1)
         pf2[rows, pl.ds(0, NX)] = re
         pf2[rows, pl.ds(NX, NX)] = im
         for c in range(2):
+            i = shot * 2 + c
             cut = slice(c * HALF, (c + 1) * HALF)
-            bq[shot * 2 + c, :, pl.ds(0, HALF)] = re[:, cut].astype(BF16)
-            bq[shot * 2 + c, :, pl.ds(HALF, HALF)] = im[:, cut].astype(BF16)
-
-    def b_send(d):
-        return remote(bq.at[y_at(d)], by.at[y], by_s.at[d - 1], by_r.at[d - 1], y_dev(d))
-
-    for d in (1, 2, 3):
-        b_send(d).start()
+            bq[i, :, pl.ds(0, HALF)] = re[:, cut].astype(BF16)
+            bq[i, :, pl.ds(HALF, HALF)] = im[:, cut].astype(BF16)
+
+            @pl.when(y != i)
+            def _(i=i):
+                b_send(i).start()
+
     by[y] = bq[y]
 
     def local_iterate(p, slot):
@@ -271,15 +297,13 @@
                 hs[slot, rows, pl.ds(0, NX)] = vr.astype(BF16)
                 hs[slot, rows, pl.ds(NX, NX)] = vi.astype(BF16)
 
+    for p in range(LZ):
+        coefficients(p)
     local_iterate(2, 0)
     halo_down = remote(hs.at[0], hr.at[0], h_s.at[0], h_r.at[0], up_dev)
     halo_up = remote(hs.at[1], hr.at[1], h_s.at[1], h_r.at[1], dn_dev)
-    halo_down.start()
-
-    exchange(0, 1)
-
-    for d in (1, 2, 3):
-        b_send(d).wait_recv()
+
+    on_others(4, y, lambda i: remote(bq.at[0], by.at[i], by_s.at[0], by_r.at[i], y_dev(1)).wait_recv())
     re, im = by[0, :, pl.ds(0, HALF)].astype(F32), by[0, :, pl.ds(HALF, HALF)].astype(F32)
     for j in range(1, 4):
         re, im = cmul(ty[j, 0], ty[j, 1], re, im)
@@ -287,17 +311,14 @@
         im = im + by[j, :, pl.ds(HALF, HALF)].astype(F32)
     for t in range(NT):
         rt, ct = slice((t // 3) * 16, (t // 3) * 16 + 16), slice((t % 3) * 128, (t % 3) * 128 + 128)
-        tot[t, 0] = re[rt, ct].astype(BF16)
-        tot[t, 1] = im[rt, ct].astype(BF16)
+        tot[t, 0] = re[rt, ct].astype(TT)
+        tot[t, 1] = im[rt, ct].astype(TT)
     for t in range(NT):
         tile_send(t, tot, ob, tot_s, tot_r)
 
-    for k in (1, 2, 3):
-        r_back(0, k).wait_recv()
-    local_iterate(0, 1)
-    halo_up.start()
-
-    exchange(1, None)
+    exchange(0)
+    f_partner(1).start()
+    exchange_far(0)
 
     def back(q):
         return remote(ibs.at[q], inb.at[own_tile], ib_s.at[q], ib_r.at[own_tile], pos_dev(q))
@@ -309,8 +330,8 @@
         cr = jnp.zeros((16, 128), F32)
         ci = jnp.zeros((16, 128), F32)
         for q in range(NPOS):
-            ibs[q, 0] = cr.astype(BF16)
-            ibs[q, 1] = ci.astype(BF16)
+            ibs[q, 0] = cr.astype(TT)
+            ibs[q, 1] = ci.astype(TT)
 
             @pl.when(pos != q)
             def _():
@@ -322,13 +343,27 @@
                 ci = ci + ob[q, 1].astype(F32)
         inb[own_tile] = ibs[pos]
 
+    exchange(1)
+    exchange_far(1)
     for k in (1, 2, 3):
-        r_back(1, k).wait_recv()
-    local_iterate(1, None)
-
-    for c in md_sends:
-        c.wait_recv()
-    coefficients(LZ)
+        r_back(0, k).wait_recv()
+    local_iterate(0, 1)
+    halo_down.start()
+    halo_up.start()
+
+    def md_send(c):
+        return remote((mass_hbm, damp_hbm)[c].at[0], md.at[c, LZ], md_s.at[0], md_r.at[0], dn_dev)
+
+    def md_forward(c):
+        return remote(md.at[c, LZ], md.at[c, LZ], md_s.at[1], md_r.at[1], shot_dev(1))
+
+    def by_core(action):
+        for c in range(2):
+            @pl.when(core == c)
+            def _(c=c):
+                action(c)
+
+    by_core(lambda c: md_send(c).start())
 
     for t in range(NT):
         @pl.when(owner(t) != pos)
@@ -356,8 +391,16 @@
         in_send(d).start()
     inc[y] = ins[y]
 
+    for k in (1, 2, 3):
+        r_back(1, k).wait_recv()
+    local_iterate(1, None)
+
+    md_send(0).wait_recv()
+    by_core(lambda c: md_forward(c).start())
     halo_down.wait_recv()
     halo_up.wait_recv()
+    md_forward(0).wait_recv()
+    coefficients(LZ)
     not_first = jnp.where(layer == 0, 0.0, 1.0).astype(F32)
     not_last = jnp.where(layer == nl - 1, 0.0, 1.0).astype(F32)
     va[0] = hr[0].astype(F32) * not_first
@@ -396,17 +439,23 @@
             c.start()
             outs.append(c)
 
+    for shot in range(2):
+        f_partner(2, shot).wait_send()
+        f_forward(2, shot).wait_send()
+        for k in (2, 3):
+            r_back(2, k, shot).wait_send()
+    for p in (0, 1):
+        f_partner(p).wait_send()
+        f_forward(p).wait_send()
+        for k in (2, 3):
+            r_back(p, k).wait_send()
     for p in order:
-        if p == 1:
-            f_partner(p).wait_send()
         f_sibling(p).wait_send()
-        f_forward(p).wait_send()
-        for k in (1, 2, 3):
-            r_back(p, k).wait_send()
-    for c in t_sends + md_sends + [halo_down, halo_up]:
+        r_back(p, 1).wait_send()
+    for c in t_sends + [halo_down, halo_up, md_send(0), md_forward(0)]:
         c.wait_send()
+    on_others(4, y, lambda i: b_send(i).wait_send())
     for d in (1, 2, 3):
-        b_send(d).wait_send()
         in_send(d).wait_send()
     for t in range(NT):
         tile_sent(t, ttile, ot, tt_s, tt_r)
@@ -424,23 +473,16 @@
 
 
 def on_device(residual_src, src_plane, src_shift, profile, mass, damping, panel, transmission):
-    vmem = pl.BlockSpec(memory_space=pltpu.VMEM)
     smem = pl.BlockSpec(memory_space=pltpu.SMEM)
     hbm = pl.BlockSpec(memory_space=pl.ANY)
-    forcing = pl.pallas_call(
-        forcing_kernel,
-        out_shape=jax.ShapeDtypeStruct((LZ, ROWS, W), BF16),
-        in_specs=[smem, smem, vmem, vmem],
-        out_specs=vmem,
-        name="forcing",
-        compiler_params=pltpu.CompilerParams(vmem_limit_bytes=16 * 2**20),
-    )(src_plane, src_shift, residual_src, profile)
     dma = pltpu.SemaphoreType.DMA
     scratch = [
+        pltpu.VMEM((2, LZ, NY, W), BF16),
+        pltpu.VMEM((2, NY, W), BF16),
         pltpu.VMEM((W, COLS), BF16),
-        pltpu.VMEM((4, LZ, ROWS, W), BF16),
-        pltpu.VMEM((4, LZ, ROWS, COLS), BF16),
-        pltpu.VMEM((LZ, 4, ROWS, COLS), BF16),
+        pltpu.VMEM((4, LZ, 2, NY, W), BF16),
+        pltpu.VMEM((4, LZ, 2, NY, COLS), BF16),
+        pltpu.VMEM((LZ, 4, 2, NY, COLS), BF16),
         pltpu.VMEM((2, LZ + 1, NY, NX), BF16),
         pltpu.VMEM((LZ + 1, 2, NY, NX), F32),
         pltpu.VMEM((NY, W), F32),
@@ -451,32 +493,32 @@
         pltpu.VMEM((ROWS, W), F32),
         pltpu.VMEM((4, NY, NX), BF16),
         pltpu.VMEM((4, NY, NX), BF16),
-        pltpu.VMEM((NT, 2, 16, 128), BF16),
-        pltpu.VMEM((NPOS, 2, 16, 128), BF16),
-        pltpu.VMEM((NPOS, 2, 16, 128), BF16),
-        pltpu.VMEM((NT, 2, 16, 128), BF16),
+        pltpu.VMEM((NT, 2, 16, 128), TT),
+        pltpu.VMEM((NPOS, 2, 16, 128), TT),
+        pltpu.VMEM((NPOS, 2, 16, 128), TT),
+        pltpu.VMEM((NT, 2, 16, 128), TT),
         pltpu.VMEM((4, NY, NX), BF16),
         pltpu.VMEM((4, NY, NX), BF16),
         pltpu.VMEM((5, ROWS, W), F32),
         pltpu.VMEM((2, ROWS, W), BF16),
         pltpu.VMEM((2, ROWS, W), BF16),
         pltpu.VMEM((2, LZ, NY, W), BF16),
-        dma((7,)), dma((LZ, 3)), dma((LZ, 3)), dma((LZ, 3)), dma((LZ, 3)), dma((2,)), dma((2,)),
+        dma((8,)), dma((LZ, 3, 2)), dma((LZ, 3, 2)), dma((LZ, 3, 2)), dma((LZ, 3, 2)), dma((2,)), dma((2,)),
         dma((3, 2)), dma((3, 2)), dma((NT,)), dma((NPOS,)),
-        dma((3,)), dma((3,)), dma((NT,)), dma((NPOS,)), dma((NPOS,)), dma((NT,)),
+        dma((4,)), dma((4,)), dma((NT,)), dma((NPOS,)), dma((NPOS,)), dma((NT,)),
         dma((3,)), dma((3,)), dma((2,)), dma((2,)), dma((2, LZ)),
     ]
     return pl.pallas_call(
         sweep_kernel,
         out_shape=jax.ShapeDtypeStruct((2, LZ, NY, W), BF16),
-        in_specs=[hbm] * 5,
+        in_specs=[smem] * 2 + [hbm] * 6,
         out_specs=hbm,
         scratch_shapes=scratch,
         name="sweep",
         compiler_params=pltpu.CompilerParams(
-            collective_id=0, has_side_effects=True, vmem_limit_bytes=40 * 2**20
+            collective_id=0, has_side_effects=True, vmem_limit_bytes=56 * 2**20
         ),
-    )(forcing, mass, damping, panel, transmission)
+    )(src_plane, src_shift, residual_src, profile, mass, damping, panel, transmission)
 
 
 def solution(mesh):

time: 78 us -> 70.7 us (0.906)
  Pallas kernels: 72.2 us -> 67.5 us
  local copies, waits for them, and re-layouts: 4.81 us -> 2.14 us
    pallas_call x1, Pallas kernels: 71.4 us -> 67.5 us  [on_device(): pl.pallas_call(sweep_kernel, out_shape=jax.ShapeDtypeStruct((2, LZ, NY, W...]
    unnamed x17 -> x1, local copies, waits for them, and re-layouts: 4.81 us -> 2.14 us
where the time goes in v2:
time: 70.7 us; the launch traced here: 69.7 us
  Pallas kernels  67.5 us (95%)
  local copies, waits for them, and re-layouts  2.14 us (3%)
    pallas_call x1, Pallas kernels, on_device(): pl.pallas_call(sweep_kernel, out_shape=jax.ShapeDtypeStruct((2, LZ, NY, W...  67.5 us
    unnamed x1, local copies, waits for them, and re-layouts  2.14 us

profile of v2, /device:TPU:1, one launch (start us, length us, event | category | flops | bytes accessed | tf_op | source)
XLA Modules:
  0.0 69.7 jit_solution(5261221624196081507)
XLA Ops:
  0.0 67.5 %sweep.1 = bf16[2,3,48,1536]{3,2,1,0:T(8,128)(2,1)} custom-call(s32[2]{0:T(128)} %plane_ref.1, s32[2]{0:T(128)} %shift_ref.1, bf16[2,3,48,1536]{3,2,1,0:T(8,128)(2,1)} %res_hbm.1, bf16[2,48,1536]{2,1,0:T(8,128)(2,1)} %prof_hbm.1, bf16[3,48,768]{2,1,0:T(8,128)(2,1)} %mass_hbm.1, bf16[3,48,768]{2,1,0:T(8,128)(2,1)} %damp_hbm.1, ...), custom_call_target="tpu_custom_call" | custom-call | tf_op jit(solution)/shard_map/sweep/pallas_call | solution.py:511
  67.5 2.1 %copy.10 = bf16[2,3,48,1536]{3,2,1,0:T(8,128)(2,1)} copy(bf16[2,3,48,1536]{3,2,1,0:T(8,128)(2,1)} %sweep.1) | data formatting | bytes 1769472

commit v3 on v2

--- a/solution.py
+++ b/solution.py
@@ -124,17 +124,13 @@
     forcing(2)
     pl.semaphore_wait(barrier, len(greet))
 
-    def f_partner(p, shot=None):
-        if shot is None:
-            return remote(fa.at[0, p], fa.at[2, p], f_s.at[p, 1, 0], f_r.at[p, 1, 0], shot_dev(2))
+    def f_partner(p, shot):
         return remote(fa.at[0, p, shot], fa.at[2, p, shot], f_s.at[p, 1, shot], f_r.at[p, 1, shot], shot_dev(2))
 
     def f_sibling(p):
         return remote(fa.at[0, p], fa.at[1, p], f_s.at[p, 0, 0], f_r.at[p, 0, 0], shot_dev(1))
 
-    def f_forward(p, shot=None):
-        if shot is None:
-            return remote(fa.at[2, p], fa.at[3, p], f_s.at[p, 2, 0], f_r.at[p, 2, 0], shot_dev(1))
+    def f_forward(p, shot):
         return remote(fa.at[2, p, shot], fa.at[3, p, shot], f_s.at[p, 2, shot], f_r.at[p, 2, shot], shot_dev(1))
 
     def r_back(p, k, shot=None):
@@ -181,24 +177,36 @@
         rs[1, p] = sib[p]
         r_back(p, 1).start()
 
-    def exchange(p, shot=None):
+    pieces = [(p, shot) for p in order for shot in range(2)]
+
+    def step(n):
+        p, shot = pieces[n]
         f_partner(p, shot).wait_recv()
         f_forward(p, shot).start()
-        where = (p,) if shot is None else (p, shot)
-        rs[(2,) + where] = product(2, p, shot)
+        if n + 2 < len(pieces):
+            f_partner(*pieces[n + 2]).start()
+        rs[2, p, shot] = product(2, p, shot)
         r_back(p, 2, shot).start()
-
-    def exchange_far(p, shot=None):
         f_forward(p, shot).wait_recv()
-        where = (p,) if shot is None else (p, shot)
-        rs[(3,) + where] = product(3, p, shot)
+        rs[3, p, shot] = product(3, p, shot)
         r_back(p, 3, shot).start()
 
-    exchange(2, 0)
-    exchange_far(2, 0)
-    exchange(2, 1)
-    f_partner(0).start()
-    exchange_far(2, 1)
+    step(0)
+    step(1)
+
+    def md_send(c):
+        return remote((mass_hbm, damp_hbm)[c].at[0], md.at[c, LZ], md_s.at[0], md_r.at[0], dn_dev)
+
+    def md_forward(c):
+        return remote(md.at[c, LZ], md.at[c, LZ], md_s.at[1], md_r.at[1], shot_dev(1))
+
+    def by_core(action):
+        for c in range(2):
+            @pl.when(core == c)
+            def _(c=c):
+                action(c)
+
+    by_core(lambda c: md_send(c).start())
 
     loads[4].wait()
     loads[5].wait()
@@ -303,6 +311,8 @@
     halo_down = remote(hs.at[0], hr.at[0], h_s.at[0], h_r.at[0], up_dev)
     halo_up = remote(hs.at[1], hr.at[1], h_s.at[1], h_r.at[1], dn_dev)
 
+    step(2)
+
     on_others(4, y, lambda i: remote(bq.at[0], by.at[i], by_s.at[0], by_r.at[i], y_dev(1)).wait_recv())
     re, im = by[0, :, pl.ds(0, HALF)].astype(F32), by[0, :, pl.ds(HALF, HALF)].astype(F32)
     for j in range(1, 4):
@@ -316,9 +326,7 @@
     for t in range(NT):
         tile_send(t, tot, ob, tot_s, tot_r)
 
-    exchange(0)
-    f_partner(1).start()
-    exchange_far(0)
+    step(3)
 
     def back(q):
         return remote(ibs.at[q], inb.at[own_tile], ib_s.at[q], ib_r.at[own_tile], pos_dev(q))
@@ -343,27 +351,20 @@
                 ci = ci + ob[q, 1].astype(F32)
         inb[own_tile] = ibs[pos]
 
-    exchange(1)
-    exchange_far(1)
-    for k in (1, 2, 3):
-        r_back(0, k).wait_recv()
+    md_send(0).wait_recv()
+    by_core(lambda c: md_forward(c).start())
+    step(4)
+    md_forward(0).wait_recv()
+    coefficients(LZ)
+
+    def products_in(p):
+        r_back(p, 1).wait_recv()
+        for shot in range(2):
+            for k in (2, 3):
+                r_back(p, k, shot).wait_recv()
+
+    products_in(0)
     local_iterate(0, 1)
-    halo_down.start()
-    halo_up.start()
-
-    def md_send(c):
-        return remote((mass_hbm, damp_hbm)[c].at[0], md.at[c, LZ], md_s.at[0], md_r.at[0], dn_dev)
-
-    def md_forward(c):
-        return remote(md.at[c, LZ], md.at[c, LZ], md_s.at[1], md_r.at[1], shot_dev(1))
-
-    def by_core(action):
-        for c in range(2):
-            @pl.when(core == c)
-            def _(c=c):
-                action(c)
-
-    by_core(lambda c: md_send(c).start())
 
     for t in range(NT):
         @pl.when(owner(t) != pos)
@@ -391,19 +392,16 @@
         in_send(d).start()
     inc[y] = ins[y]
 
-    for k in (1, 2, 3):
-        r_back(1, k).wait_recv()
+    step(5)
+    halo_down.start()
+    halo_up.start()
+
+    products_in(1)
     local_iterate(1, None)
 
-    md_send(0).wait_recv()
-    by_core(lambda c: md_forward(c).start())
-    halo_down.wait_recv()
-    halo_up.wait_recv()
-    md_forward(0).wait_recv()
-    coefficients(LZ)
     not_first = jnp.where(layer == 0, 0.0, 1.0).astype(F32)
     not_last = jnp.where(layer == nl - 1, 0.0, 1.0).astype(F32)
-    va[0] = hr[0].astype(F32) * not_first
+    rcols, icols = pl.ds(0, NX), pl.ds(NX, NX)
 
     for d in (1, 2, 3):
         in_send(d).wait_recv()
@@ -412,43 +410,49 @@
         re = jnp.concatenate([inc[shot * 2 + c, :, pl.ds(0, HALF)] for c in range(2)], axis=-1).astype(F32)
         im = jnp.concatenate([inc[shot * 2 + c, :, pl.ds(HALF, HALF)] for c in range(2)], axis=-1).astype(F32)
         vr, vi = cmul(coef[0, 0], coef[0, 1], re, im)
-        rcols, icols = pl.ds(0, NX), pl.ds(NX, NX)
         va[1, rows, rcols] += vr
         va[1, rows, icols] += vi
         nr, ni = cmul(tv[:, rcols], tv[:, icols], re, im)
         nr = nr + pf2[rows, rcols]
         ni = ni + pf2[rows, icols]
         vr, vi = cmul(coef[LZ, 0], coef[LZ, 1], nr, ni)
-        va[4, rows, rcols] = (vr + hr[1, rows, rcols].astype(F32)) * not_last
-        va[4, rows, icols] = (vi + hr[1, rows, icols].astype(F32)) * not_last
+        va[4, rows, rcols] = vr
+        va[4, rows, icols] = vi
 
     outs = []
-    for p in range(LZ):
+
+    def finish(p):
         for shot in range(2):
             rows = pl.ds(shot * NY, NY)
             diff = []
             for part in range(2):
                 cols = pl.ds(part * NX, NX)
                 mid = va[p + 1, rows, cols]
-                w = mid + 0.5 * (va[p, rows, cols] + va[p + 2, rows, cols])
+                above, below = va[p, rows, cols], va[p + 2, rows, cols]
+                if p == 0:
+                    above = hr[0, rows, cols].astype(F32) * not_first
+                if p == LZ - 1:
+                    below = (below + hr[1, rows, cols].astype(F32)) * not_last
+                w = mid + 0.5 * (above + below)
                 diff.append(lateral(w) - mid)
             dr, di = cmul(coef[p, 0], coef[p, 1], diff[0], diff[1])
-            outv[shot, p, :, pl.ds(0, NX)] = (1.2 * va[p + 1, rows, pl.ds(0, NX)] + dr * (1.0 / 7.0)).astype(BF16)
-            outv[shot, p, :, pl.ds(NX, NX)] = (1.2 * va[p + 1, rows, pl.ds(NX, NX)] + di * (1.0 / 7.0)).astype(BF16)
+            outv[shot, p, :, rcols] = (1.2 * va[p + 1, rows, rcols] + dr * (1.0 / 7.0)).astype(BF16)
+            outv[shot, p, :, icols] = (1.2 * va[p + 1, rows, icols] + di * (1.0 / 7.0)).astype(BF16)
             c = pltpu.make_async_copy(outv.at[shot, p], out_hbm.at[shot, p], out_s.at[shot, p])
             c.start()
             outs.append(c)
 
-    for shot in range(2):
-        f_partner(2, shot).wait_send()
-        f_forward(2, shot).wait_send()
+    finish(1)
+    halo_down.wait_recv()
+    finish(0)
+    halo_up.wait_recv()
+    finish(2)
+
+    for p, shot in pieces:
+        f_partner(p, shot).wait_send()
+        f_forward(p, shot).wait_send()
         for k in (2, 3):
-            r_back(2, k, shot).wait_send()
-    for p in (0, 1):
-        f_partner(p).wait_send()
-        f_forward(p).wait_send()
-        for k in (2, 3):
-            r_back(p, k).wait_send()
+            r_back(p, k, shot).wait_send()
     for p in order:
         f_sibling(p).wait_send()
         r_back(p, 1).wait_send()
@@ -474,7 +478,7 @@
 
 def on_device(residual_src, src_plane, src_shift, profile, mass, damping, panel, transmission):
     smem = pl.BlockSpec(memory_space=pltpu.SMEM)
-    hbm = pl.BlockSpec(memory_space=pl.ANY)
+    hbm = pl.BlockSpec(memory_space=pltpu.HBM)
     dma = pltpu.SemaphoreType.DMA
     scratch = [
         pltpu.VMEM((2, LZ, NY, W), BF16),
@@ -512,7 +516,7 @@
         sweep_kernel,
         out_shape=jax.ShapeDtypeStruct((2, LZ, NY, W), BF16),
         in_specs=[smem] * 2 + [hbm] * 6,
-        out_specs=hbm,
+        out_specs=pl.BlockSpec(memory_space=pl.ANY),
         scratch_shapes=scratch,
         name="sweep",
         compiler_params=pltpu.CompilerParams(

time: 70.7 us -> 65.7 us (0.929); the launches traced: 69.7 us -> 65.6 us
  Pallas kernels: 67.5 us -> 63.5 us
    pallas_call x1, Pallas kernels: 67.5 us -> 63.5 us  [on_device(): pl.pallas_call(sweep_kernel, out_shape=jax.ShapeDtypeStruct((2, LZ, NY, W...]
where the time goes in v3:
time: 65.7 us; the launch traced here: 65.6 us
  Pallas kernels  63.5 us (97%)
  local copies, waits for them, and re-layouts  2.14 us (3%)
    pallas_call x1, Pallas kernels, on_device(): pl.pallas_call(sweep_kernel, out_shape=jax.ShapeDtypeStruct((2, LZ, NY, W...  63.5 us
    unnamed x1, local copies, waits for them, and re-layouts  2.14 us

profile of v3, /device:TPU:1, one launch (start us, length us, event | category | flops | bytes accessed | tf_op | source)
XLA Modules:
  0.0 65.6 jit_solution(7201349786724054195)
XLA Ops:
  0.0 63.5 %sweep.1 = bf16[2,3,48,1536]{3,2,1,0:T(8,128)(2,1)} custom-call(s32[2]{0:T(128)} %plane_ref.1, s32[2]{0:T(128)} %shift_ref.1, bf16[2,3,48,1536]{3,2,1,0:T(8,128)(2,1)} %res_hbm.1, bf16[2,48,1536]{2,1,0:T(8,128)(2,1)} %prof_hbm.1, bf16[3,48,768]{2,1,0:T(8,128)(2,1)} %mass_hbm.1, bf16[3,48,768]{2,1,0:T(8,128)(2,1)} %damp_hbm.1, ...), custom_call_target="tpu_custom_call" | custom-call | tf_op jit(solution)/shard_map/sweep/pallas_call | solution.py:515
  63.5 2.1 %copy.10 = bf16[2,3,48,1536]{3,2,1,0:T(8,128)(2,1)} copy(bf16[2,3,48,1536]{3,2,1,0:T(8,128)(2,1)} %sweep.1) | data formatting | bytes 1769472

commit v4 on v3

--- a/solution.py
+++ b/solution.py
@@ -8,6 +8,8 @@
 MESH = pl.DeviceIdType.MESH
 F32, BF16 = jnp.float32, jnp.bfloat16
 RELAX = 0.8
+ISSUE = ((), (2,), (), (), (), ())
+LATE = ((), (3,), (4,), (5,), (), ())
 TT = BF16
 NY, NX, W, LZ = 48, 768, 1536, 3
 ROWS = 2 * NY
@@ -183,13 +185,15 @@
         p, shot = pieces[n]
         f_partner(p, shot).wait_recv()
         f_forward(p, shot).start()
-        if n + 2 < len(pieces):
-            f_partner(*pieces[n + 2]).start()
+        for m in ISSUE[n]:
+            f_partner(*pieces[m]).start()
         rs[2, p, shot] = product(2, p, shot)
         r_back(p, 2, shot).start()
         f_forward(p, shot).wait_recv()
         rs[3, p, shot] = product(3, p, shot)
         r_back(p, 3, shot).start()
+        for m in LATE[n]:
+            f_partner(*pieces[m]).start()
 
     step(0)
     step(1)
@@ -217,6 +221,62 @@
         w = RELAX / (sh * sh + dm * dm)
         coef[p, 0] = w * sh
         coef[p, 1] = -(w * dm)
+
+    def tile_send(t, src, dst, ss, rsem):
+        @pl.when(owner(t) != pos)
+        def _():
+            remote(src.at[t], dst.at[pos], ss.at[t], rsem.at[pos], pos_dev(owner(t))).start()
+
+        @pl.when(owner(t) == pos)
+        def _():
+            dst[pos] = src[t]
+
+    def tile_sent(t, src, dst, ss, rsem):
+        @pl.when(owner(t) != pos)
+        def _():
+            remote(src.at[t], dst.at[pos], ss.at[t], rsem.at[pos], pos_dev(owner(t))).wait_send()
+
+    def tile_recv(src, dst, ss, rsem):
+        for q in range(NPOS):
+            @pl.when(pos != q)
+            def _():
+                remote(src.at[0], dst.at[q], ss.at[0], rsem.at[q], pos_dev(q)).wait_recv()
+
+
+    def field(p, shot, part):
+        f = fa[0, p, shot, :, pl.ds(part * NX, NX)].astype(F32)
+        prod = jnp.concatenate([rr[p, part * 2, shot], rr[p, part * 2 + 1, shot]], axis=-1)
+        return f + prod.astype(F32)
+
+    def b_send(i):
+        return remote(bq.at[i], by.at[y], by_s.at[i], by_r.at[y], ((layer // 4) * 4 + i, s))
+
+    def on_others(n, mine, action):
+        for i in range(n):
+            @pl.when(mine != i)
+            def _(i=i):
+                action(i)
+
+    for shot in range(2):
+        rows = pl.ds(shot * NY, NY)
+        if shot == 0:
+            r_back(2, 1).wait_recv()
+        for k in (2, 3):
+            r_back(2, k, shot).wait_recv()
+        re, im = field(2, shot, 0), field(2, shot, 1)
+        pf2[rows, pl.ds(0, NX)] = re
+        pf2[rows, pl.ds(NX, NX)] = im
+        for c in range(2):
+            i = shot * 2 + c
+            cut = slice(c * HALF, (c + 1) * HALF)
+            bq[i, :, pl.ds(0, HALF)] = re[:, cut].astype(BF16)
+            bq[i, :, pl.ds(HALF, HALF)] = im[:, cut].astype(BF16)
+
+            @pl.when(y != i)
+            def _(i=i):
+                b_send(i).start()
+
+    by[y] = bq[y]
 
     loads[3].wait()
     loads[6].wait()
@@ -233,63 +293,8 @@
         for part in range(2):
             ttile[t, part] = tblk[part, rt, ct]
 
-    def tile_send(t, src, dst, ss, rsem):
-        @pl.when(owner(t) != pos)
-        def _():
-            remote(src.at[t], dst.at[pos], ss.at[t], rsem.at[pos], pos_dev(owner(t))).start()
-
-        @pl.when(owner(t) == pos)
-        def _():
-            dst[pos] = src[t]
-
-    def tile_sent(t, src, dst, ss, rsem):
-        @pl.when(owner(t) != pos)
-        def _():
-            remote(src.at[t], dst.at[pos], ss.at[t], rsem.at[pos], pos_dev(owner(t))).wait_send()
-
-    def tile_recv(src, dst, ss, rsem):
-        for q in range(NPOS):
-            @pl.when(pos != q)
-            def _():
-                remote(src.at[0], dst.at[q], ss.at[0], rsem.at[q], pos_dev(q)).wait_recv()
-
     for t in range(NT):
         tile_send(t, ttile, ot, tt_s, tt_r)
-
-    def field(p, shot, part):
-        f = fa[0, p, shot, :, pl.ds(part * NX, NX)].astype(F32)
-        prod = jnp.concatenate([rr[p, part * 2, shot], rr[p, part * 2 + 1, shot]], axis=-1)
-        return f + prod.astype(F32)
-
-    def b_send(i):
-        return remote(bq.at[i], by.at[y], by_s.at[i], by_r.at[y], ((layer // 4) * 4 + i, s))
-
-    def on_others(n, mine, action):
-        for i in range(n):
-            @pl.when(mine != i)
-            def _(i=i):
-                action(i)
-
-    for shot in range(2):
-        rows = pl.ds(shot * NY, NY)
-        if shot == 0:
-            r_back(2, 1).wait_recv()
-        for k in (2, 3):
-            r_back(2, k, shot).wait_recv()
-        re, im = field(2, shot, 0), field(2, shot, 1)
-        pf2[rows, pl.ds(0, NX)] = re
-        pf2[rows, pl.ds(NX, NX)] = im
-        for c in range(2):
-            i = shot * 2 + c
-            cut = slice(c * HALF, (c + 1) * HALF)
-            bq[i, :, pl.ds(0, HALF)] = re[:, cut].astype(BF16)
-            bq[i, :, pl.ds(HALF, HALF)] = im[:, cut].astype(BF16)
-
-            @pl.when(y != i)
-            def _(i=i):
-                b_send(i).start()
-
-    by[y] = bq[y]
 
     def local_iterate(p, slot):
         for shot in range(2):

time: 65.7 us -> 63.9 us (0.973)
  Pallas kernels: 63.5 us -> 61.6 us
    pallas_call x1, Pallas kernels: 63.5 us -> 61.6 us  [on_device(): pl.pallas_call(sweep_kernel, out_shape=jax.ShapeDtypeStruct((2, LZ, NY, W...]
where the time goes in v4:
time: 63.9 us; the launch traced here: 63.7 us
  Pallas kernels  61.6 us (96%)
  local copies, waits for them, and re-layouts  2.14 us (3%)
    pallas_call x1, Pallas kernels, on_device(): pl.pallas_call(sweep_kernel, out_shape=jax.ShapeDtypeStruct((2, LZ, NY, W...  61.6 us
    unnamed x1, local copies, waits for them, and re-layouts  2.14 us

profile of v4, /device:TPU:1, one launch (start us, length us, event | category | flops | bytes accessed | tf_op | source)
XLA Modules:
  0.0 63.7 jit_solution(6765677068339240836)
XLA Ops:
  0.0 61.6 %sweep.1 = bf16[2,3,48,1536]{3,2,1,0:T(8,128)(2,1)} custom-call(s32[2]{0:T(128)} %plane_ref.1, s32[2]{0:T(128)} %shift_ref.1, bf16[2,3,48,1536]{3,2,1,0:T(8,128)(2,1)} %res_hbm.1, bf16[2,48,1536]{2,1,0:T(8,128)(2,1)} %prof_hbm.1, bf16[3,48,768]{2,1,0:T(8,128)(2,1)} %mass_hbm.1, bf16[3,48,768]{2,1,0:T(8,128)(2,1)} %damp_hbm.1, ...), custom_call_target="tpu_custom_call" | custom-call | tf_op jit(solution)/shard_map/sweep/pallas_call | solution.py:520
  61.6 2.1 %copy.10 = bf16[2,3,48,1536]{3,2,1,0:T(8,128)(2,1)} copy(bf16[2,3,48,1536]{3,2,1,0:T(8,128)(2,1)} %sweep.1) | data formatting | bytes 1769472
